TPU v7x, 512 devices: a whole 4x8x8 slice. The times are simulated.
512 devices in a mesh: dp: 16 (over y, core), ctx: 32 (over z, x).
Axes of the slice: x: 4, y: 8, z: 8, core: 2. Of those that a mesh axis runs over, the one named last changes fastest.
Arguments:
- query_rows: bfloat16 [65536, 2048], P(('dp', 'ctx')), parts along dimension 0, may hold values from -130 to 130
- key_token_rows: bfloat16 [65536, 512], P(('dp', 'ctx')), parts along dimension 0, may hold values from -4 to 4
- value_token_rows: bfloat16 [65536, 512], P(('dp', 'ctx')), parts along dimension 0, may hold values from -6 to 6
- doc_lengths: int32 [256], P('dp'), parts along dimension 0, may hold values from 1 to 1536, 4096 in all
Outputs:
- attended: bfloat16 [65536, 2048], P(('dp', 'ctx')), parts along dimension 0
There are 16 independent parts, one for each index of `dp`. A program takes and returns all parts, laid end to end along the dimension named above; each array names one. Nothing has to cross between parts.
Inputs may be any that keep to these rules, and one draw needn't show every extreme that they name: `doc_lengths`: each sequence's lengths sum to 4096; the longest document has exactly 1536 tokens.
All inputs are finite; a program needn't handle non-finite values.
Results may differ from a plain program's by a relative error of at most 0.0044.
Values may be sent and summed in bfloat16 or wider, within the bound.
A program may use at most 128 MiB of HBM per device.

v0:
```python
import jax
import jax.numpy as jnp
from jax import lax
from jax.sharding import PartitionSpec as P

HEAD_SIZE = 128


def passed_along(shard, axis, by):
    size = lax.axis_size(axis)
    pairs = [(i, i + by) for i in range(size) if 0 <= i + by < size]
    return lax.ppermute(shard, axis, pairs)


def doc_index(positions, bounds):
    return jnp.sum((positions[:, None] >= bounds[None, :]).astype(jnp.int32), axis=1)


def update(state, query_tile_rows, key_head_split, value_head_split, allowed, score_scale):
    run_max, run_sum, run_acc = state
    scores = (
        jnp.einsum(
            "qkgd,tkd->kgqt", query_tile_rows, key_head_split, preferred_element_type=jnp.float32
        )
        * score_scale
    )
    scores = jnp.where(allowed[None, None], scores, -jnp.inf)
    new_max = jnp.maximum(run_max, jnp.max(scores, axis=-1))
    safe_max = jnp.where(jnp.isfinite(new_max), new_max, jnp.float32(0.0))
    factor = jnp.exp(run_max - safe_max)
    expo = jnp.exp(scores - safe_max[..., None])
    new_sum = run_sum * factor + jnp.sum(expo, axis=-1)
    weights = expo.astype(jnp.bfloat16)
    new_acc = run_acc * factor[..., None] + jnp.einsum(
        "kgqt,tkd->kgqd", weights, value_head_split, preferred_element_type=jnp.float32
    )
    return (new_max, new_sum, new_acc)


def body(query_rows, key_token_rows, value_token_rows, doc_lengths):
    ctx_count = lax.axis_size("ctx")
    own_index = lax.axis_index("ctx")
    local_rows = query_rows.shape[0]
    half_rows = local_rows // 2
    head_dim = HEAD_SIZE
    kv_heads = key_token_rows.shape[1] // head_dim
    queries_per_group = query_rows.shape[1] // key_token_rows.shape[1]
    score_scale = head_dim ** (-0.5)
    bounds = jnp.cumsum(doc_lengths)
    first_start = own_index * local_rows
    second_block = query_rows[half_rows:]
    second_start = first_start + half_rows
    query_blocks = (
        query_rows[:half_rows].reshape(half_rows, kv_heads, queries_per_group, head_dim),
        second_block.reshape(half_rows, kv_heads, queries_per_group, head_dim),
    )
    query_pos = (
        first_start + jnp.arange(half_rows, dtype=jnp.int32),
        second_start + jnp.arange(half_rows, dtype=jnp.int32),
    )
    query_doc = (doc_index(query_pos[0], bounds), doc_index(query_pos[1], bounds))

    def accumulate(running, pieces, piece_start):
        key_piece, value_piece = pieces
        count = key_piece.shape[0]
        key_pos = piece_start + jnp.arange(count, dtype=jnp.int32)
        key_doc = doc_index(key_pos, bounds)
        key_head_split = key_piece.reshape(count, kv_heads, head_dim)
        value_head_split = value_piece.reshape(count, kv_heads, head_dim)
        results = []
        for group_number in range(2):
            allowed = (
                (key_pos[None, :] >= 0)
                & (key_pos[None, :] <= query_pos[group_number][:, None])
                & (key_doc[None, :] == query_doc[group_number][:, None])
            )
            block = query_blocks[group_number]

            def compute(state, block=block, allowed=allowed):
                return update(state, block, key_head_split, value_head_split, allowed, score_scale)

            def keep(state):
                return state

            results.append(lax.cond(jnp.any(allowed), compute, keep, running[group_number]))
        return (results[0], results[1])

    starting = (
        jnp.full((kv_heads, queries_per_group, half_rows), -jnp.inf, jnp.float32),
        jnp.zeros((kv_heads, queries_per_group, half_rows), jnp.float32),
        jnp.zeros((kv_heads, queries_per_group, half_rows, head_dim), jnp.float32),
    )
    total_rows = ctx_count * local_rows
    longest = 3 * total_rows // 8
    reach = min(ctx_count - 1, max(1, -(-(longest - 1) // local_rows)))
    stacked = jnp.stack((key_token_rows, value_token_rows))
    own_state = accumulate((starting, starting), (key_token_rows, value_token_rows), first_start)

    def window_step(step, carry):
        moving, state = carry
        moving = passed_along(moving, "ctx", 1)
        piece_start = first_start - step * local_rows
        state = accumulate(state, (moving[0], moving[1]), piece_start)
        return (moving, state)

    moved, finished = lax.fori_loop(1, reach + 1, window_step, (stacked, own_state))
    outputs = []
    for group_number in range(2):
        run_max, run_sum, run_acc = finished[group_number]
        mixed = run_acc / run_sum[..., None]
        outputs.append(
            jnp.transpose(mixed, (2, 0, 1, 3)).reshape(half_rows, -1).astype(jnp.bfloat16)
        )
    second_out = outputs[1]
    return jnp.concatenate([outputs[0], second_out], axis=0)


def solution(mesh):
    in_specs = (P(("dp", "ctx"), None), P(("dp", "ctx"), None), P(("dp", "ctx"), None), P("dp"))
    out_specs = P(("dp", "ctx"), None)
    return jax.shard_map(body, mesh=mesh, in_specs=in_specs, out_specs=out_specs, check_vma=False)
```

profile of v0, /device:TPU:304, one launch (start us, length us, event | category | flops | bytes accessed | tf_op | source)
XLA Modules:
  0.0 188.8 jit_solution(16693498624861714633)
XLA Ops:
  5.0 1.7 conditional.4
  6.8 1.7 conditional.5
  8.5 178.3 %while.27 = (s32[]{:T(128)}, bf16[2,128,512]{2,1,0:T(8,128)(2,1)S(1)}, f32[4,4,64]{2,1,0:T(4,128)S(1)}, f32[4,4,64]{2,1,0:T(4,128)S(1)}, f32[4,4,64,128]{3,2,1,0...) while((s32[]{:T(128)}, ...), condition=%wide.region_26.27_spmd.clone.clone, body=%wide.region_14.26_spmd.clone.clone.sunk | while | flops 136677760 | bytes 9089817 | solution.py:106
  8.5 3.4 %collective-permute-start = (bf16[2,128,512]{2,1,0:T(8,128)(2,1)S(1)}, bf16[2,128,512]{2,1,0:T(8,128)(2,1)S(1)}, u32[]{:S(2)}, u32[]{:S(2)}) collective-permute-start(bf16[2,128,512]{2,1,0:T(8,128)(2,1)S(1)} %get-tuple-element.784), channel_id=1, source_target_pairs={{0,1},{1,2},{2,3},{3,4},{4,5},{5,6},{6,7},{7,8},{8,9},{9,10},{10,1... | collective-permute-start | bytes 786440 | tf_op jit(solution)/shard_map/while/body/eval_jaxpr/ppermute | solution.py:12
  14.1 7.6 %collective-permute-done = bf16[2,128,512]{2,1,0:T(8,128)(2,1)S(1)} collective-permute-done((bf16[2,128,512]{2,1,0:T(8,128)(2,1)S(1)}, bf16[2,128,512]{2,1,0:T(8,128)(2,1)S(1)}, u32[]{:S(2)}, u32[]{:S(2)}) %collective-permute-start) | collective-permute-done | bytes 262176 | tf_op jit(solution)/shard_map/while/body/eval_jaxpr/ppermute | solution.py:12
  21.8 1.4 conditional.12
  23.2 1.4 conditional.13
  24.7 1.9 %collective-permute-start = (bf16[2,128,512]{2,1,0:T(8,128)(2,1)S(1)}, bf16[2,128,512]{2,1,0:T(8,128)(2,1)S(1)}, u32[]{:S(2)}, u32[]{:S(2)}) collective-permute-start(bf16[2,128,512]{2,1,0:T(8,128)(2,1)S(1)} %get-tuple-element.784), channel_id=1, source_target_pairs={{0,1},{1,2},{2,3},{3,4},{4,5},{5,6},{6,7},{7,8},{8,9},{9,10},{10,1... | collective-permute-start | bytes 786440 | tf_op jit(solution)/shard_map/while/body/eval_jaxpr/ppermute | solution.py:12
  28.9 8.2 %collective-permute-done = bf16[2,128,512]{2,1,0:T(8,128)(2,1)S(1)} collective-permute-done((bf16[2,128,512]{2,1,0:T(8,128)(2,1)S(1)}, bf16[2,128,512]{2,1,0:T(8,128)(2,1)S(1)}, u32[]{:S(2)}, u32[]{:S(2)}) %collective-permute-start) | collective-permute-done | bytes 262176 | tf_op jit(solution)/shard_map/while/body/eval_jaxpr/ppermute | solution.py:12
  37.2 1.4 conditional.12
  38.7 1.4 conditional.13
  40.2 1.9 %collective-permute-start = (bf16[2,128,512]{2,1,0:T(8,128)(2,1)S(1)}, bf16[2,128,512]{2,1,0:T(8,128)(2,1)S(1)}, u32[]{:S(2)}, u32[]{:S(2)}) collective-permute-start(bf16[2,128,512]{2,1,0:T(8,128)(2,1)S(1)} %get-tuple-element.784), channel_id=1, source_target_pairs={{0,1},{1,2},{2,3},{3,4},{4,5},{5,6},{6,7},{7,8},{8,9},{9,10},{10,1... | collective-permute-start | bytes 786440 | tf_op jit(solution)/shard_map/while/body/eval_jaxpr/ppermute | solution.py:12
  44.3 7.4 %collective-permute-done = bf16[2,128,512]{2,1,0:T(8,128)(2,1)S(1)} collective-permute-done((bf16[2,128,512]{2,1,0:T(8,128)(2,1)S(1)}, bf16[2,128,512]{2,1,0:T(8,128)(2,1)S(1)}, u32[]{:S(2)}, u32[]{:S(2)}) %collective-permute-start) | collective-permute-done | bytes 262176 | tf_op jit(solution)/shard_map/while/body/eval_jaxpr/ppermute | solution.py:12
  51.8 1.4 conditional.12
  53.3 1.4 conditional.13
  54.8 1.9 %collective-permute-start = (bf16[2,128,512]{2,1,0:T(8,128)(2,1)S(1)}, bf16[2,128,512]{2,1,0:T(8,128)(2,1)S(1)}, u32[]{:S(2)}, u32[]{:S(2)}) collective-permute-start(bf16[2,128,512]{2,1,0:T(8,128)(2,1)S(1)} %get-tuple-element.784), channel_id=1, source_target_pairs={{0,1},{1,2},{2,3},{3,4},{4,5},{5,6},{6,7},{7,8},{8,9},{9,10},{10,1... | collective-permute-start | bytes 786440 | tf_op jit(solution)/shard_map/while/body/eval_jaxpr/ppermute | solution.py:12
  58.9 7.4 %collective-permute-done = bf16[2,128,512]{2,1,0:T(8,128)(2,1)S(1)} collective-permute-done((bf16[2,128,512]{2,1,0:T(8,128)(2,1)S(1)}, bf16[2,128,512]{2,1,0:T(8,128)(2,1)S(1)}, u32[]{:S(2)}, u32[]{:S(2)}) %collective-permute-start) | collective-permute-done | bytes 262176 | tf_op jit(solution)/shard_map/while/body/eval_jaxpr/ppermute | solution.py:12
  66.5 1.4 conditional.12
  67.9 1.4 conditional.13
  69.4 1.9 %collective-permute-start = (bf16[2,128,512]{2,1,0:T(8,128)(2,1)S(1)}, bf16[2,128,512]{2,1,0:T(8,128)(2,1)S(1)}, u32[]{:S(2)}, u32[]{:S(2)}) collective-permute-start(bf16[2,128,512]{2,1,0:T(8,128)(2,1)S(1)} %get-tuple-element.784), channel_id=1, source_target_pairs={{0,1},{1,2},{2,3},{3,4},{4,5},{5,6},{6,7},{7,8},{8,9},{9,10},{10,1... | collective-permute-start | bytes 786440 | tf_op jit(solution)/shard_map/while/body/eval_jaxpr/ppermute | solution.py:12
  73.5 7.6 %collective-permute-done = bf16[2,128,512]{2,1,0:T(8,128)(2,1)S(1)} collective-permute-done((bf16[2,128,512]{2,1,0:T(8,128)(2,1)S(1)}, bf16[2,128,512]{2,1,0:T(8,128)(2,1)S(1)}, u32[]{:S(2)}, u32[]{:S(2)}) %collective-permute-start) | collective-permute-done | bytes 262176 | tf_op jit(solution)/shard_map/while/body/eval_jaxpr/ppermute | solution.py:12
  81.2 1.4 conditional.12
  82.7 1.4 conditional.13
  84.2 1.9 %collective-permute-start = (bf16[2,128,512]{2,1,0:T(8,128)(2,1)S(1)}, bf16[2,128,512]{2,1,0:T(8,128)(2,1)S(1)}, u32[]{:S(2)}, u32[]{:S(2)}) collective-permute-start(bf16[2,128,512]{2,1,0:T(8,128)(2,1)S(1)} %get-tuple-element.784), channel_id=1, source_target_pairs={{0,1},{1,2},{2,3},{3,4},{4,5},{5,6},{6,7},{7,8},{8,9},{9,10},{10,1... | collective-permute-start | bytes 786440 | tf_op jit(solution)/shard_map/while/body/eval_jaxpr/ppermute | solution.py:12
  88.3 8.9 %collective-permute-done = bf16[2,128,512]{2,1,0:T(8,128)(2,1)S(1)} collective-permute-done((bf16[2,128,512]{2,1,0:T(8,128)(2,1)S(1)}, bf16[2,128,512]{2,1,0:T(8,128)(2,1)S(1)}, u32[]{:S(2)}, u32[]{:S(2)}) %collective-permute-start) | collective-permute-done | bytes 262176 | tf_op jit(solution)/shard_map/while/body/eval_jaxpr/ppermute | solution.py:12
  97.3 1.4 conditional.12
  98.8 1.4 conditional.13
  100.3 1.9 %collective-permute-start = (bf16[2,128,512]{2,1,0:T(8,128)(2,1)S(1)}, bf16[2,128,512]{2,1,0:T(8,128)(2,1)S(1)}, u32[]{:S(2)}, u32[]{:S(2)}) collective-permute-start(bf16[2,128,512]{2,1,0:T(8,128)(2,1)S(1)} %get-tuple-element.784), channel_id=1, source_target_pairs={{0,1},{1,2},{2,3},{3,4},{4,5},{5,6},{6,7},{7,8},{8,9},{9,10},{10,1... | collective-permute-start | bytes 786440 | tf_op jit(solution)/shard_map/while/body/eval_jaxpr/ppermute | solution.py:12
  104.4 7.4 %collective-permute-done = bf16[2,128,512]{2,1,0:T(8,128)(2,1)S(1)} collective-permute-done((bf16[2,128,512]{2,1,0:T(8,128)(2,1)S(1)}, bf16[2,128,512]{2,1,0:T(8,128)(2,1)S(1)}, u32[]{:S(2)}, u32[]{:S(2)}) %collective-permute-start) | collective-permute-done | bytes 262176 | tf_op jit(solution)/shard_map/while/body/eval_jaxpr/ppermute | solution.py:12
  112.0 1.4 conditional.12
  113.4 1.4 conditional.13
  114.9 1.9 %collective-permute-start = (bf16[2,128,512]{2,1,0:T(8,128)(2,1)S(1)}, bf16[2,128,512]{2,1,0:T(8,128)(2,1)S(1)}, u32[]{:S(2)}, u32[]{:S(2)}) collective-permute-start(bf16[2,128,512]{2,1,0:T(8,128)(2,1)S(1)} %get-tuple-element.784), channel_id=1, source_target_pairs={{0,1},{1,2},{2,3},{3,4},{4,5},{5,6},{6,7},{7,8},{8,9},{9,10},{10,1... | collective-permute-start | bytes 786440 | tf_op jit(solution)/shard_map/while/body/eval_jaxpr/ppermute | solution.py:12
  119.0 8.6 %collective-permute-done = bf16[2,128,512]{2,1,0:T(8,128)(2,1)S(1)} collective-permute-done((bf16[2,128,512]{2,1,0:T(8,128)(2,1)S(1)}, bf16[2,128,512]{2,1,0:T(8,128)(2,1)S(1)}, u32[]{:S(2)}, u32[]{:S(2)}) %collective-permute-start) | collective-permute-done | bytes 262176 | tf_op jit(solution)/shard_map/while/body/eval_jaxpr/ppermute | solution.py:12
  127.7 1.4 conditional.12
  129.2 1.4 conditional.13
  130.7 1.9 %collective-permute-start = (bf16[2,128,512]{2,1,0:T(8,128)(2,1)S(1)}, bf16[2,128,512]{2,1,0:T(8,128)(2,1)S(1)}, u32[]{:S(2)}, u32[]{:S(2)}) collective-permute-start(bf16[2,128,512]{2,1,0:T(8,128)(2,1)S(1)} %get-tuple-element.784), channel_id=1, source_target_pairs={{0,1},{1,2},{2,3},{3,4},{4,5},{5,6},{6,7},{7,8},{8,9},{9,10},{10,1... | collective-permute-start | bytes 786440 | tf_op jit(solution)/shard_map/while/body/eval_jaxpr/ppermute | solution.py:12
  134.8 7.9 %collective-permute-done = bf16[2,128,512]{2,1,0:T(8,128)(2,1)S(1)} collective-permute-done((bf16[2,128,512]{2,1,0:T(8,128)(2,1)S(1)}, bf16[2,128,512]{2,1,0:T(8,128)(2,1)S(1)}, u32[]{:S(2)}, u32[]{:S(2)}) %collective-permute-start) | collective-permute-done | bytes 262176 | tf_op jit(solution)/shard_map/while/body/eval_jaxpr/ppermute | solution.py:12
  142.8 1.4 conditional.12
  144.3 1.4 conditional.13
  145.8 1.9 %collective-permute-start = (bf16[2,128,512]{2,1,0:T(8,128)(2,1)S(1)}, bf16[2,128,512]{2,1,0:T(8,128)(2,1)S(1)}, u32[]{:S(2)}, u32[]{:S(2)}) collective-permute-start(bf16[2,128,512]{2,1,0:T(8,128)(2,1)S(1)} %get-tuple-element.784), channel_id=1, source_target_pairs={{0,1},{1,2},{2,3},{3,4},{4,5},{5,6},{6,7},{7,8},{8,9},{9,10},{10,1... | collective-permute-start | bytes 786440 | tf_op jit(solution)/shard_map/while/body/eval_jaxpr/ppermute | solution.py:12
  149.9 7.4 %collective-permute-done = bf16[2,128,512]{2,1,0:T(8,128)(2,1)S(1)} collective-permute-done((bf16[2,128,512]{2,1,0:T(8,128)(2,1)S(1)}, bf16[2,128,512]{2,1,0:T(8,128)(2,1)S(1)}, u32[]{:S(2)}, u32[]{:S(2)}) %collective-permute-start) | collective-permute-done | bytes 262176 | tf_op jit(solution)/shard_map/while/body/eval_jaxpr/ppermute | solution.py:12
  157.4 1.4 conditional.12
  160.4 1.9 %collective-permute-start = (bf16[2,128,512]{2,1,0:T(8,128)(2,1)S(1)}, bf16[2,128,512]{2,1,0:T(8,128)(2,1)S(1)}, u32[]{:S(2)}, u32[]{:S(2)}) collective-permute-start(bf16[2,128,512]{2,1,0:T(8,128)(2,1)S(1)} %get-tuple-element.784), channel_id=1, source_target_pairs={{0,1},{1,2},{2,3},{3,4},{4,5},{5,6},{6,7},{7,8},{8,9},{9,10},{10,1... | collective-permute-start | bytes 786440 | tf_op jit(solution)/shard_map/while/body/eval_jaxpr/ppermute | solution.py:12
  164.5 7.4 %collective-permute-done = bf16[2,128,512]{2,1,0:T(8,128)(2,1)S(1)} collective-permute-done((bf16[2,128,512]{2,1,0:T(8,128)(2,1)S(1)}, bf16[2,128,512]{2,1,0:T(8,128)(2,1)S(1)}, u32[]{:S(2)}, u32[]{:S(2)}) %collective-permute-start) | collective-permute-done | bytes 262176 | tf_op jit(solution)/shard_map/while/body/eval_jaxpr/ppermute | solution.py:12
  172.1 1.4 conditional.12
  173.5 1.4 conditional.13
  175.0 1.9 %collective-permute-start = (bf16[2,128,512]{2,1,0:T(8,128)(2,1)S(1)}, bf16[2,128,512]{2,1,0:T(8,128)(2,1)S(1)}, u32[]{:S(2)}, u32[]{:S(2)}) collective-permute-start(bf16[2,128,512]{2,1,0:T(8,128)(2,1)S(1)} %get-tuple-element.784), channel_id=1, source_target_pairs={{0,1},{1,2},{2,3},{3,4},{4,5},{5,6},{6,7},{7,8},{8,9},{9,10},{10,1... | collective-permute-start | bytes 786440 | tf_op jit(solution)/shard_map/while/body/eval_jaxpr/ppermute | solution.py:12
  179.1 7.4 %collective-permute-done = bf16[2,128,512]{2,1,0:T(8,128)(2,1)S(1)} collective-permute-done((bf16[2,128,512]{2,1,0:T(8,128)(2,1)S(1)}, bf16[2,128,512]{2,1,0:T(8,128)(2,1)S(1)}, u32[]{:S(2)}, u32[]{:S(2)}) %collective-permute-start) | collective-permute-done | bytes 262176 | tf_op jit(solution)/shard_map/while/body/eval_jaxpr/ppermute | solution.py:12
  (293 shorter events, 53.0 us)
Async XLA Ops:
  0.0 0.7 copy-start.7
  2.5 1.9 %copy-start.6 = (bf16[128,512]{1,0:T(8,128)(2,1)S(1)}, bf16[128,512]{1,0:T(8,128)(2,1)}, u32[]{:S(2)}) copy-start(bf16[128,512]{1,0:T(8,128)(2,1)} %param.15) | copy-start | bytes 393220
  3.2 1.1 copy-start.5
  3.2 1.3 copy-start.4
  5.4 0.6 copy-start
  6.1 0.7 copy-start.1
  7.1 0.6 copy-start.2
  7.8 0.7 copy-start.3
  8.5 13.2 %collective-permute-start = (bf16[2,128,512]{2,1,0:T(8,128)(2,1)S(1)}, bf16[2,128,512]{2,1,0:T(8,128)(2,1)S(1)}, u32[]{:S(2)}, u32[]{:S(2)}) collective-permute-start(bf16[2,128,512]{2,1,0:T(8,128)(2,1)S(1)} %get-tuple-element.784), channel_id=1, source_target_pairs={{0,1},{1,2},{2,3},{3,4},{4,5},{5,6},{6,7},{7,8},{8,9},{9,10},{10,1... | collective-permute-start | bytes 786440 | tf_op jit(solution)/shard_map/while/body/eval_jaxpr/ppermute | solution.py:12
  24.7 12.4 %collective-permute-start = (bf16[2,128,512]{2,1,0:T(8,128)(2,1)S(1)}, bf16[2,128,512]{2,1,0:T(8,128)(2,1)S(1)}, u32[]{:S(2)}, u32[]{:S(2)}) collective-permute-start(bf16[2,128,512]{2,1,0:T(8,128)(2,1)S(1)} %get-tuple-element.784), channel_id=1, source_target_pairs={{0,1},{1,2},{2,3},{3,4},{4,5},{5,6},{6,7},{7,8},{8,9},{9,10},{10,1... | collective-permute-start | bytes 786440 | tf_op jit(solution)/shard_map/while/body/eval_jaxpr/ppermute | solution.py:12
  40.2 11.6 %collective-permute-start = (bf16[2,128,512]{2,1,0:T(8,128)(2,1)S(1)}, bf16[2,128,512]{2,1,0:T(8,128)(2,1)S(1)}, u32[]{:S(2)}, u32[]{:S(2)}) collective-permute-start(bf16[2,128,512]{2,1,0:T(8,128)(2,1)S(1)} %get-tuple-element.784), channel_id=1, source_target_pairs={{0,1},{1,2},{2,3},{3,4},{4,5},{5,6},{6,7},{7,8},{8,9},{9,10},{10,1... | collective-permute-start | bytes 786440 | tf_op jit(solution)/shard_map/while/body/eval_jaxpr/ppermute | solution.py:12
  54.8 11.6 %collective-permute-start = (bf16[2,128,512]{2,1,0:T(8,128)(2,1)S(1)}, bf16[2,128,512]{2,1,0:T(8,128)(2,1)S(1)}, u32[]{:S(2)}, u32[]{:S(2)}) collective-permute-start(bf16[2,128,512]{2,1,0:T(8,128)(2,1)S(1)} %get-tuple-element.784), channel_id=1, source_target_pairs={{0,1},{1,2},{2,3},{3,4},{4,5},{5,6},{6,7},{7,8},{8,9},{9,10},{10,1... | collective-permute-start | bytes 786440 | tf_op jit(solution)/shard_map/while/body/eval_jaxpr/ppermute | solution.py:12
  69.4 11.8 %collective-permute-start = (bf16[2,128,512]{2,1,0:T(8,128)(2,1)S(1)}, bf16[2,128,512]{2,1,0:T(8,128)(2,1)S(1)}, u32[]{:S(2)}, u32[]{:S(2)}) collective-permute-start(bf16[2,128,512]{2,1,0:T(8,128)(2,1)S(1)} %get-tuple-element.784), channel_id=1, source_target_pairs={{0,1},{1,2},{2,3},{3,4},{4,5},{5,6},{6,7},{7,8},{8,9},{9,10},{10,1... | collective-permute-start | bytes 786440 | tf_op jit(solution)/shard_map/while/body/eval_jaxpr/ppermute | solution.py:12
  84.2 13.1 %collective-permute-start = (bf16[2,128,512]{2,1,0:T(8,128)(2,1)S(1)}, bf16[2,128,512]{2,1,0:T(8,128)(2,1)S(1)}, u32[]{:S(2)}, u32[]{:S(2)}) collective-permute-start(bf16[2,128,512]{2,1,0:T(8,128)(2,1)S(1)} %get-tuple-element.784), channel_id=1, source_target_pairs={{0,1},{1,2},{2,3},{3,4},{4,5},{5,6},{6,7},{7,8},{8,9},{9,10},{10,1... | collective-permute-start | bytes 786440 | tf_op jit(solution)/shard_map/while/body/eval_jaxpr/ppermute | solution.py:12
  100.3 11.6 %collective-permute-start = (bf16[2,128,512]{2,1,0:T(8,128)(2,1)S(1)}, bf16[2,128,512]{2,1,0:T(8,128)(2,1)S(1)}, u32[]{:S(2)}, u32[]{:S(2)}) collective-permute-start(bf16[2,128,512]{2,1,0:T(8,128)(2,1)S(1)} %get-tuple-element.784), channel_id=1, source_target_pairs={{0,1},{1,2},{2,3},{3,4},{4,5},{5,6},{6,7},{7,8},{8,9},{9,10},{10,1... | collective-permute-start | bytes 786440 | tf_op jit(solution)/shard_map/while/body/eval_jaxpr/ppermute | solution.py:12
  114.9 12.7 %collective-permute-start = (bf16[2,128,512]{2,1,0:T(8,128)(2,1)S(1)}, bf16[2,128,512]{2,1,0:T(8,128)(2,1)S(1)}, u32[]{:S(2)}, u32[]{:S(2)}) collective-permute-start(bf16[2,128,512]{2,1,0:T(8,128)(2,1)S(1)} %get-tuple-element.784), channel_id=1, source_target_pairs={{0,1},{1,2},{2,3},{3,4},{4,5},{5,6},{6,7},{7,8},{8,9},{9,10},{10,1... | collective-permute-start | bytes 786440 | tf_op jit(solution)/shard_map/while/body/eval_jaxpr/ppermute | solution.py:12
  130.7 12.1 %collective-permute-start = (bf16[2,128,512]{2,1,0:T(8,128)(2,1)S(1)}, bf16[2,128,512]{2,1,0:T(8,128)(2,1)S(1)}, u32[]{:S(2)}, u32[]{:S(2)}) collective-permute-start(bf16[2,128,512]{2,1,0:T(8,128)(2,1)S(1)} %get-tuple-element.784), channel_id=1, source_target_pairs={{0,1},{1,2},{2,3},{3,4},{4,5},{5,6},{6,7},{7,8},{8,9},{9,10},{10,1... | collective-permute-start | bytes 786440 | tf_op jit(solution)/shard_map/while/body/eval_jaxpr/ppermute | solution.py:12
  145.8 11.6 %collective-permute-start = (bf16[2,128,512]{2,1,0:T(8,128)(2,1)S(1)}, bf16[2,128,512]{2,1,0:T(8,128)(2,1)S(1)}, u32[]{:S(2)}, u32[]{:S(2)}) collective-permute-start(bf16[2,128,512]{2,1,0:T(8,128)(2,1)S(1)} %get-tuple-element.784), channel_id=1, source_target_pairs={{0,1},{1,2},{2,3},{3,4},{4,5},{5,6},{6,7},{7,8},{8,9},{9,10},{10,1... | collective-permute-start | bytes 786440 | tf_op jit(solution)/shard_map/while/body/eval_jaxpr/ppermute | solution.py:12
  160.4 11.6 %collective-permute-start = (bf16[2,128,512]{2,1,0:T(8,128)(2,1)S(1)}, bf16[2,128,512]{2,1,0:T(8,128)(2,1)S(1)}, u32[]{:S(2)}, u32[]{:S(2)}) collective-permute-start(bf16[2,128,512]{2,1,0:T(8,128)(2,1)S(1)} %get-tuple-element.784), channel_id=1, source_target_pairs={{0,1},{1,2},{2,3},{3,4},{4,5},{5,6},{6,7},{7,8},{8,9},{9,10},{10,1... | collective-permute-start | bytes 786440 | tf_op jit(solution)/shard_map/while/body/eval_jaxpr/ppermute | solution.py:12
  175.0 11.6 %collective-permute-start = (bf16[2,128,512]{2,1,0:T(8,128)(2,1)S(1)}, bf16[2,128,512]{2,1,0:T(8,128)(2,1)S(1)}, u32[]{:S(2)}, u32[]{:S(2)}) collective-permute-start(bf16[2,128,512]{2,1,0:T(8,128)(2,1)S(1)} %get-tuple-element.784), channel_id=1, source_target_pairs={{0,1},{1,2},{2,3},{3,4},{4,5},{5,6},{6,7},{7,8},{8,9},{9,10},{10,1... | collective-permute-start | bytes 786440 | tf_op jit(solution)/shard_map/while/body/eval_jaxpr/ppermute | solution.py:12
where the time goes:
time: 190 us; the launch traced here: 189 us
  waiting for transfers between devices  93.6 us (49%)
  starting transfers between devices  24.5 us (13%)
  other arithmetic  23.6 us (12%)
  matrix products  22.3 us (12%)
  loops' own time  17.7 us (9%)
  local copies, waits for them, and re-layouts  5.66 us (3%)
    ppermute x12, waiting for transfers between devices, passed_along(): return lax.ppermute(shard, axis, pairs)  93.6 us
    ppermute x12, starting transfers between devices, passed_along(): return lax.ppermute(shard, axis, pairs)  24.5 us
    another operation x1, loops' own time, body(): lax.fori_loop(1, reach + 1, window_step, (stacked, own_state))  16.4 us
    dot_general x24, matrix products, update(): jnp.einsum('kgqt,tkd->kgqd', weights, value_head_split, preferred_element...  13.2 us
    reduce_or x13, other arithmetic, accumulate(): jnp.any(allowed)  10.4 us
    reduce_sum x24, other arithmetic, update(): new_sum = run_sum * factor + jnp.sum(expo, axis=-1)  9.76 us
    dot_general x24, matrix products, update(): jnp.einsum('qkgd,tkd->kgqt', query_tile_rows, key_head_split, preferred_e...  9.13 us
  transfers between devices with their start and end apart: 12, of which 12 were waited for; matrix products, arithmetic and copies ran while one was open for 6% of the time, Pallas kernels for 0%

commit v1 on v0

v1 whole, which is shorter than its diff:
```python
import math

import jax
import jax.numpy as jnp
from jax import lax
from jax.experimental import pallas as pl
from jax.experimental.pallas import tpu as pltpu
from jax.sharding import PartitionSpec as P

HEAD = 128
ROWS = 128
SIDE = 4
REACH = 3
LANES = 128
MESH = pl.DeviceIdType.MESH
LOWEST = -1e30
RATE = math.log2(math.e) / math.sqrt(HEAD)


def kernel(
    lengths, q_hbm, k_hbm, v_hbm, out_hbm,
    q_buf, kv, lo_ref, top, total, acc, o_stage,
    loc_sem, x_send, x_recv, q_send, q_recv, z_send, z_recv, o_send, o_recv, o_loc,
):
    me = lax.axis_index("ctx")
    count = lax.axis_size("ctx")
    z, x = me // SIDE, me % SIDE
    base = z * SIDE

    def mate(d):
        return base + (x + d) % SIDE

    above = (me + SIDE) % count
    below = (me + count - SIDE) % count

    def head_cols(ref, head, width):
        return ref.at[:, pl.ds(pl.multiple_of(head * width, width), width)]

    local = [
        pltpu.make_async_copy(head_cols(k_hbm, x, HEAD), kv.at[0, x, 0], loc_sem.at[0]),
        pltpu.make_async_copy(head_cols(v_hbm, x, HEAD), kv.at[0, x, 1], loc_sem.at[1]),
        pltpu.make_async_copy(head_cols(q_hbm, x, SIDE * HEAD), q_buf.at[x], loc_sem.at[2]),
    ]
    for copy in local:
        copy.start()

    barrier = pltpu.get_barrier_semaphore()
    for other in (mate(1), mate(2), mate(3), above, below):
        pl.semaphore_signal(barrier, inc=1, device_id={"ctx": other}, device_id_type=MESH)

    def starts(b, carry):
        pos = (base + b) * ROWS + lax.broadcasted_iota(jnp.int32, (ROWS, LANES), 0)
        lo = jnp.zeros((ROWS, LANES), jnp.int32)
        bound = jnp.int32(0)
        for i in range(lengths.shape[0]):
            bound = bound + lengths[i]
            lo = jnp.where(pos >= bound, bound, lo)
        lo_ref[b] = lo
        return carry

    lax.fori_loop(0, SIDE, starts, 0)
    pl.semaphore_wait(barrier, 5)

    def remote(src, dst, send, recv, to):
        return pltpu.make_async_remote_copy(
            src_ref=src, dst_ref=dst, send_sem=send, recv_sem=recv,
            device_id={"ctx": to}, device_id_type=MESH,
        )

    kv_x = {}
    for d in (1, 3, 2):
        to = (x + d) % SIDE
        kv_x[d] = [
            remote(head_cols(ref, to, HEAD), kv.at[0, x, j], x_send.at[d - 1, j], x_recv.at[d - 1, j], mate(d))
            for j, ref in enumerate((k_hbm, v_hbm))
        ]
        for copy in kv_x[d]:
            copy.start()

    def hop(row, piece, slot):
        return remote(kv.at[row, piece], kv.at[row + 1, piece], z_send.at[row, slot], z_recv.at[row, slot], above)

    order = [(x, 0), ((x + 3) % SIDE, 1), ((x + 1) % SIDE, 3), ((x + 2) % SIDE, 2)]
    local[0].wait()
    local[1].wait()
    hops = []
    for slot, (piece, d) in enumerate(order):
        if d:
            for copy in kv_x[d]:
                copy.wait_recv()
        copy = hop(0, piece, slot)
        copy.start()
        hops.append(copy)
        if slot == 0:
            q_x = {}
            for d2 in (1, 3, 2):
                q_x[d2] = remote(
                    head_cols(q_hbm, (x + d2) % SIDE, SIDE * HEAD), q_buf.at[x],
                    q_send.at[d2 - 1], q_recv.at[d2 - 1], mate(d2),
                )
                q_x[d2].start()
    local[2].wait()
    for d in (1, 3, 2):
        q_x[d].wait_recv()

    def attend(b, row, first_piece, pieces, first=False):
        n = pieces * ROWS
        q = q_buf[b]
        q4 = jnp.concatenate([q[:, h * HEAD:(h + 1) * HEAD] for h in range(SIDE)], axis=0)
        k = kv[row, pl.ds(first_piece, pieces), 0].reshape(n, HEAD)
        v = kv[row, pl.ds(first_piece, pieces), 1].reshape(n, HEAD)
        s4 = lax.dot_general(q4, k, (((1,), (1,)), ((), ())), preferred_element_type=jnp.float32)
        key_pos = (base - row * SIDE + first_piece) * ROWS + lax.broadcasted_iota(jnp.int32, (ROWS, n), 1)
        lo = jnp.concatenate([lo_ref[b]] * pieces, axis=1)
        allowed = key_pos >= lo
        if first:
            q_pos = (base + b) * ROWS + lax.broadcasted_iota(jnp.int32, (ROWS, n), 0)
            allowed = allowed & (key_pos <= q_pos)
        for h in range(SIDE):
            at = pl.ds(h * ROWS, ROWS)
            s = jnp.where(allowed, s4[h * ROWS:(h + 1) * ROWS], LOWEST)
            peak = jnp.broadcast_to(jnp.max(s, axis=1, keepdims=True), (ROWS, LANES))
            if not first:
                old = top[b, at]
                peak = jnp.maximum(old, peak)
                fade = jnp.exp2((old - peak) * RATE)
            expo = jnp.exp2((s - jnp.concatenate([peak] * pieces, axis=1)) * RATE)
            sums = jnp.broadcast_to(jnp.sum(expo, axis=1, keepdims=True), (ROWS, LANES))
            mixed = jnp.dot(expo.astype(jnp.bfloat16), v, preferred_element_type=jnp.float32)
            if first:
                total[b, at] = sums
                acc[b, at] = mixed
            else:
                total[b, at] = total[b, at] * fade + sums
                acc[b, at] = acc[b, at] * fade + mixed
            top[b, at] = peak

    def whole_row(row, first=False):
        def step(b, carry):
            attend(b, row, 0, SIDE, first)
            return carry

        lax.fori_loop(0, SIDE, step, 0)

    whole_row(0, True)

    for slot, (piece, d) in enumerate(order):
        hops[slot].wait_recv()
        copy = hop(1, piece, slot)
        copy.start()
        hops.append(copy)
    whole_row(1)
    for slot in range(SIDE):
        hops[SIDE + slot].wait_recv()
    last = []
    for slot, piece in enumerate((3, 2, 1, 0)):
        copy = hop(2, piece, slot)
        copy.start()
        last.append(copy)
    whole_row(2)

    outs = []
    for slot, b in enumerate((3, 2, 1, 0)):
        if b == 0:
            attend(b, 3, 1, 3)
        last[slot].wait_recv()
        if b == 0:
            attend(b, 3, 0, 1)
        else:
            attend(b, 3, b, SIDE - b)
        for h in range(SIDE):
            at = pl.ds(h * ROWS, ROWS)
            o_stage[b, :, h * HEAD:(h + 1) * HEAD] = (acc[b, at] / total[b, at]).astype(jnp.bfloat16)
        d = (b + SIDE - x) % SIDE
        home = head_cols(out_hbm, x, SIDE * HEAD)
        away = remote(o_stage.at[b], home, o_send.at[b], o_recv.at[x], base + b)
        stay = pltpu.make_async_copy(o_stage.at[b], home, o_loc)
        outs.append((b, away, stay))

        @pl.when(x == b)
        def _():
            stay.start()

        @pl.when(x != b)
        def _():
            away.start()

    for b, away, stay in outs:
        @pl.when(x == b)
        def _():
            stay.wait()

        @pl.when(x != b)
        def _():
            away.wait_send()

    for b in range(SIDE):
        @pl.when(x != b)
        def _():
            remote(
                o_stage.at[b], head_cols(out_hbm, b, SIDE * HEAD), o_send.at[b], o_recv.at[b], base + b
            ).wait_recv()

    for d in (1, 2, 3):
        for copy in kv_x[d]:
            copy.wait_send()
        q_x[d].wait_send()
    for copy in hops + last:
        copy.wait_send()


def body(q, k, v, lengths):
    any_spec = pl.BlockSpec(memory_space=pl.ANY)
    dma = pltpu.SemaphoreType.DMA
    return pl.pallas_call(
        kernel,
        out_shape=jax.ShapeDtypeStruct(q.shape, jnp.bfloat16),
        in_specs=[pl.BlockSpec(memory_space=pltpu.SMEM), any_spec, any_spec, any_spec],
        out_specs=any_spec,
        scratch_shapes=[
            pltpu.VMEM((SIDE, ROWS, SIDE * HEAD), jnp.bfloat16),
            pltpu.VMEM((REACH + 1, SIDE, 2, ROWS, HEAD), jnp.bfloat16),
            pltpu.VMEM((SIDE, ROWS, LANES), jnp.int32),
            pltpu.VMEM((SIDE, SIDE * ROWS, LANES), jnp.float32),
            pltpu.VMEM((SIDE, SIDE * ROWS, LANES), jnp.float32),
            pltpu.VMEM((SIDE, SIDE * ROWS, HEAD), jnp.float32),
            pltpu.VMEM((SIDE, ROWS, SIDE * HEAD), jnp.bfloat16),
            dma((3,)), dma((3, 2)), dma((3, 2)), dma((3,)), dma((3,)),
            dma((REACH, SIDE)), dma((REACH, SIDE)), dma((SIDE,)), dma((SIDE,)), dma(()),
        ],
        compiler_params=pltpu.CompilerParams(
            collective_id=0, has_side_effects=True, vmem_limit_bytes=40 * 1024 * 1024
        ),
        name="attention",
    )(lengths, q, k, v)


def solution(mesh):
    in_specs = (P(("dp", "ctx"), None), P(("dp", "ctx"), None), P(("dp", "ctx"), None), P("dp"))
    out_specs = P(("dp", "ctx"), None)
    return jax.shard_map(body, mesh=mesh, in_specs=in_specs, out_specs=out_specs, check_vma=False)
```

time: 190 us -> 49 us (0.26)
  the two profiles are of different devices: /device:TPU:304 before, /device:TPU:56 now
where the time goes in v1:
time: 49 us; the launch traced here: 48.8 us
  Pallas kernels  44.5 us (91%)
  local copies, waits for them, and re-layouts  4.3 us (9%)
    pallas_call x1, Pallas kernels, body(): pl.pallas_call(kernel, out_shape=jax.ShapeDtypeStruct(q.shape, jnp.bfloat...  44.5 us
    unnamed x9, local copies, waits for them, and re-layouts  4.3 us

profile of v1, /device:TPU:56, one launch (start us, length us, event | category | flops | bytes accessed | tf_op | source)
XLA Modules:
  0.0 48.8 jit_solution(17043299292644699362)
XLA Ops:
  0.0 0.0 copy-start
  0.0 1.0 %copy-done = bf16[128,2048]{1,0:T(8,128)(2,1)S(1)} copy-done((bf16[128,2048]{1,0:T(8,128)(2,1)S(1)}, bf16[128,2048]{1,0:T(8,128)(2,1)}, u32[]{:S(2)}) %copy-start) | copy-done | bytes 524312
  1.0 0.0 copy-start.1
  1.0 0.9 %copy-done.1 = bf16[128,512]{1,0:T(8,128)(2,1)S(1)} copy-done((bf16[128,512]{1,0:T(8,128)(2,1)S(1)}, bf16[128,512]{1,0:T(8,128)(2,1)}, u32[]{:S(2)}) %copy-start.1) | copy-done | bytes 131096
  1.9 0.0 copy-start.2
  1.9 0.9 %copy-done.2 = bf16[128,512]{1,0:T(8,128)(2,1)S(1)} copy-done((bf16[128,512]{1,0:T(8,128)(2,1)S(1)}, bf16[128,512]{1,0:T(8,128)(2,1)}, u32[]{:S(2)}) %copy-start.2) | copy-done | bytes 131096
  2.9 0.0 copy-start.3
  2.9 0.7 %copy-done.3 = s32[16]{0:T(128)S(1)} copy-done((s32[16]{0:T(128)S(1)}, s32[16]{0:T(128)}, u32[]{:S(2)}) %copy-start.3) | copy-done | bytes 88
  3.5 44.5 %attention.1 = bf16[128,2048]{1,0:T(8,128)(2,1)S(1)} custom-call(s32[16]{0:T(128)S(1)} %copy-done.3, bf16[128,2048]{1,0:T(8,128)(2,1)S(1)} %copy-done, bf16[128,512]{1,0:T(8,128)(2,1)S(1)} %copy-done.1, bf16[128,512]{1,0:T(8,128)(2,1)S(1)} %copy-done.2), custom_call_target="tpu_custom_call" | custom-call | tf_op jit(solution)/shard_map/attention/pallas_call | solution.py:215
  48.0 0.8 %copy.6 = bf16[128,2048]{1,0:T(8,128)(2,1)} copy(bf16[128,2048]{1,0:T(8,128)(2,1)S(1)} %attention.1) | data formatting | bytes 1048576
Async XLA Ops:
  0.0 1.0 %copy-start = (bf16[128,2048]{1,0:T(8,128)(2,1)S(1)}, bf16[128,2048]{1,0:T(8,128)(2,1)}, u32[]{:S(2)}) copy-start(bf16[128,2048]{1,0:T(8,128)(2,1)} %q_hbm.1) | copy-start | bytes 1572868
  1.0 0.9 %copy-start.1 = (bf16[128,512]{1,0:T(8,128)(2,1)S(1)}, bf16[128,512]{1,0:T(8,128)(2,1)}, u32[]{:S(2)}) copy-start(bf16[128,512]{1,0:T(8,128)(2,1)} %k_hbm.1) | copy-start | bytes 393220
  1.9 0.9 %copy-start.2 = (bf16[128,512]{1,0:T(8,128)(2,1)S(1)}, bf16[128,512]{1,0:T(8,128)(2,1)}, u32[]{:S(2)}) copy-start(bf16[128,512]{1,0:T(8,128)(2,1)} %v_hbm.1) | copy-start | bytes 393220
  2.9 0.7 %copy-start.3 = (s32[16]{0:T(128)S(1)}, s32[16]{0:T(128)}, u32[]{:S(2)}) copy-start(s32[16]{0:T(128)} %lengths.1) | copy-start | bytes 196

commit v2 on v1

v2 whole, which is shorter than its diff:
```python
import math

import jax
import jax.numpy as jnp
from jax import lax
from jax.experimental import pallas as pl
from jax.experimental.pallas import tpu as pltpu
from jax.sharding import PartitionSpec as P

HEAD = 128
ROWS = 128
SIDE = 4
REACH = 3
LANES = 128
WIDE = SIDE * HEAD
MESH = pl.DeviceIdType.MESH
LOWEST = -1e30
RATE = math.log2(math.e) / math.sqrt(HEAD)


def kernel(
    lengths_hbm, q_hbm, k_hbm, v_hbm, out_hbm,
    lengths, q_buf, kv, lo_ref, top, total, acc, o_stage,
    loc_sem, x_send, x_recv, z_send, z_recv, o_send, o_recv,
):
    me = lax.axis_index("ctx")
    count = lax.axis_size("ctx")
    depth = count // SIDE
    z, x = me // SIDE, me % SIDE
    base = z * SIDE
    left, right, far = (x + 3) % SIDE, (x + 1) % SIDE, (x + 2) % SIDE
    above = (me + SIDE) % count
    below = (me + count - SIDE) % count

    def held(row, piece):
        return (REACH - row) * SIDE + piece

    def cols(ref, head, width, start=0, rows=ROWS):
        return ref.at[pl.ds(start, rows), pl.ds(pl.multiple_of(head * width, width), width)]

    local = [
        pltpu.make_async_copy(cols(k_hbm, x, HEAD), kv.at[held(0, x), 0], loc_sem.at[0]),
        pltpu.make_async_copy(cols(v_hbm, x, HEAD), kv.at[held(0, x), 1], loc_sem.at[1]),
        pltpu.make_async_copy(lengths_hbm, lengths, loc_sem.at[2]),
        pltpu.make_async_copy(cols(q_hbm, x, WIDE), q_buf.at[x], loc_sem.at[3]),
    ]
    for copy in local:
        copy.start()

    barrier = pltpu.get_barrier_semaphore()

    def greet(other):
        pl.semaphore_signal(barrier, inc=1, device_id={"ctx": other}, device_id_type=MESH)

    for mate in (left, right, far):
        greet(base + mate)
    pl.when(z > 0)(lambda: greet(below))
    pl.when(z < depth - 1)(lambda: greet(above))

    pl.semaphore_wait(barrier, 3 + jnp.where(z > 0, 1, 0) + jnp.where(z < depth - 1, 1, 0))

    def remote(src, dst, send, recv, to):
        return pltpu.make_async_remote_copy(
            src_ref=src, dst_ref=dst, send_sem=send, recv_sem=recv,
            device_id={"ctx": to}, device_id_type=MESH,
        )

    def x_copy(slot, src, dst, to):
        return remote(src, dst, x_send.at[slot], x_recv.at[slot], base + to)

    def pair(slot, to):
        return [
            x_copy(slot, cols(k_hbm, to, HEAD), kv.at[held(0, x), 0], to),
            x_copy(slot + 1, cols(v_hbm, to, HEAD), kv.at[held(0, x), 1], to),
        ]

    kv_out = {"right": pair(0, right), "left": pair(2, left), "far": pair(4, far)}
    q_out = {
        "right": x_copy(6, cols(q_hbm, right, WIDE), q_buf.at[x], right),
        "left": x_copy(7, cols(q_hbm, left, WIDE), q_buf.at[x], left),
        "far": x_copy(8, cols(q_hbm, far, WIDE), q_buf.at[x], far),
    }
    for copy in kv_out["right"] + kv_out["left"]:
        copy.start()
    for copy in kv_out["far"]:
        copy.start()

    class Hop:
        def __init__(self, row, piece, slot):
            self.row = row
            self.copy = remote(
                kv.at[held(row, piece)], kv.at[held(row + 1, piece)], z_send.at[row, slot], z_recv.at[row, slot], above
            )
            self.sends = (z >= row) & (z < depth - 1)

        def start(self):
            pl.when(self.sends)(self.copy.start)

        def wait_send(self):
            pl.when(self.sends)(self.copy.wait_send)

        def wait_recv(self):
            pl.when(z > self.row)(self.copy.wait_recv)

    order = (
        (x, left, right, far),
        (x, left, jnp.maximum(right, far), jnp.minimum(right, far)),
        (3, 2, 1, 0),
    )
    hops = [[Hop(row, piece, slot) for slot, piece in enumerate(order[row])] for row in range(REACH)]

    local[0].wait()
    local[1].wait()
    hops[0][0].start()
    def clear(b, carry):
        top[b] = jnp.full((WIDE, LANES), LOWEST, jnp.float32)
        total[b] = jnp.zeros((WIDE, LANES), jnp.float32)
        acc[b] = jnp.zeros((WIDE, HEAD), jnp.float32)
        return carry

    lax.fori_loop(0, SIDE, clear, 0)

    def blank(i, carry):
        kv[i] = jnp.zeros((2, ROWS, HEAD), jnp.bfloat16)
        return carry

    lax.fori_loop(0, SIDE * jnp.maximum(REACH - z, 0), blank, 0)
    local[2].wait()

    def starts(b, carry):
        pos = (base + b) * ROWS + lax.broadcasted_iota(jnp.int32, (ROWS, LANES), 0)
        lo = jnp.zeros((ROWS, LANES), jnp.int32)
        bound = jnp.int32(0)
        for i in range(lengths.shape[0]):
            bound = bound + lengths[i]
            lo = jnp.where(pos >= bound, bound, lo)
        lo_ref[b] = lo
        return carry

    lax.fori_loop(0, SIDE, starts, 0)
    for copy in kv_out["right"]:
        copy.wait_recv()
    hops[0][1].start()
    for copy in kv_out["left"]:
        copy.wait_recv()
    hops[0][2].start()
    for copy in q_out.values():
        copy.start()
    for copy in kv_out["far"]:
        copy.wait_recv()
    hops[0][3].start()
    for slot in (0, 1):
        hops[0][slot].wait_recv()
        hops[1][slot].start()
    local[3].wait()

    def attend(b, first, pieces, causal=False):
        n = pieces * ROWS
        heads = [pl.ds(h * ROWS, ROWS) for h in range(SIDE)]
        q = q_buf[b]
        q4 = jnp.concatenate([q[:, h * HEAD:(h + 1) * HEAD] for h in range(SIDE)], axis=0)
        k = kv[pl.ds(first, pieces), 0].reshape(n, HEAD)
        v = kv[pl.ds(first, pieces), 1].reshape(n, HEAD)
        s4 = lax.dot_general(q4, k, (((1,), (1,)), ((), ())), preferred_element_type=jnp.float32)
        start = (base - REACH * SIDE + first) * ROWS
        key_pos = start + lax.broadcasted_iota(jnp.int32, (ROWS, n), 1)
        allowed = key_pos >= jnp.concatenate([lo_ref[b]] * pieces, axis=1)
        if causal:
            allowed = allowed & (key_pos <= (base + b) * ROWS + lax.broadcasted_iota(jnp.int32, (ROWS, n), 0))
        olds = [(top[b, at], total[b, at], acc[b, at]) for at in heads]
        news = []
        for h, (old_top, old_total, old_acc) in enumerate(olds):
            s = jnp.where(allowed, s4[h * ROWS:(h + 1) * ROWS], LOWEST)
            peak = jnp.maximum(old_top, jnp.broadcast_to(jnp.max(s, axis=1, keepdims=True), (ROWS, LANES)))
            fade = jnp.exp2((old_top - peak) * RATE)
            expo = jnp.exp2((s - jnp.concatenate([peak] * pieces, axis=1)) * RATE)
            sums = old_total * fade
            for i in range(pieces):
                sums = sums + expo[:, i * LANES:(i + 1) * LANES]
            mixed = jnp.dot(expo.astype(jnp.bfloat16), v, preferred_element_type=jnp.float32)
            news.append((peak, sums, old_acc * fade + mixed))
        for at, (peak, sums, mixed) in zip(heads, news):
            top[b, at] = peak
            total[b, at] = sums
            acc[b, at] = mixed

    def finish(b):
        for h in range(SIDE):
            at = pl.ds(h * ROWS, ROWS)
            sums = jnp.broadcast_to(jnp.sum(total[b, at], axis=1, keepdims=True), (ROWS, LANES))
            o_stage[b, :, h * HEAD:(h + 1) * HEAD] = (acc[b, at] / sums).astype(jnp.bfloat16)

    def block(step, carry):
        @pl.when(step == 0)
        def _():
            for slot in (2, 3):
                hops[0][slot].wait_recv()
            for slot in (2, 3):
                hops[1][slot].start()

        @pl.when(step == 1)
        def _():
            q_out["right"].wait_recv()

        @pl.when(step == 2)
        def _():
            q_out["left"].wait_recv()

        @pl.when(step == 3)
        def _():
            q_out["far"].wait_recv()
            for slot in (0, 1, 2):
                hops[1][slot].wait_recv()
            hops[2][0].start()

        shift = jnp.where(step == 0, 0, jnp.where(step == 1, 3, step - 1))
        attend((x + shift) % SIDE, 2 * SIDE, 2 * SIDE, True)
        return carry

    lax.fori_loop(0, SIDE, block, 0)
    hops[1][3].wait_recv()
    for slot in (1, 2, 3):
        hops[2][slot].start()

    def o_copy(kind, b, src, dst, to):
        return remote(src, dst, o_send.at[kind, b], o_recv.at[kind, b], base + to)

    def output(b, name):
        near = cols(out_hbm, x, WIDE)
        return {
            "stay": lambda: pltpu.make_async_copy(o_stage.at[b], near, loc_sem.at[0]),
            "right": lambda: o_copy(0, b, o_stage.at[b], near, right),
            "left": lambda: o_copy(1, b, o_stage.at[b], near, left),
            "far": lambda: o_copy(2, b, o_stage.at[b], near, far),
        }[name]()

    @pl.when(z >= 2)
    def _():
        def ahead(b, carry):
            attend(b, SIDE, SIDE)
            return carry

        lax.fori_loop(0, 2, ahead, 0)

    for slot, b in enumerate((3, 2, 1, 0)):
        if b == 0:
            pl.when(z >= REACH)(lambda: attend(b, 1, SIDE - 1))
        hops[2][slot].wait_recv()
        if b == 0:
            pl.when(z >= REACH)(lambda: attend(b, 0, 1))
        elif b == 1:
            pl.when(z >= REACH)(lambda: attend(b, 1, SIDE - 1))
        else:
            pl.when(z >= 2)(lambda: attend(b, b, 2 * SIDE - b))
        finish(b)
        pl.when(x == b)(lambda: output(b, "stay").start())
        pl.when(right == b)(lambda: output(b, "right").start())
        pl.when(left == b)(lambda: output(b, "left").start())
        pl.when(far == b)(lambda: output(b, "far").start())

    for name in ("right", "left", "far"):
        output(x, name).wait_recv()
    output(x, "stay").wait()
    output(right, "right").wait_send()
    output(left, "left").wait_send()
    output(far, "far").wait_send()
    for copies in (*kv_out.values(), q_out.values(), *hops):
        for copy in copies:
            copy.wait_send()


def body(q, k, v, lengths):
    far_spec = pl.BlockSpec(memory_space=pltpu.HBM)
    dma = pltpu.SemaphoreType.DMA
    q, k, v, lengths = (pltpu.with_memory_space_constraint(a, pltpu.HBM) for a in (q, k, v, lengths))
    return pl.pallas_call(
        kernel,
        out_shape=jax.ShapeDtypeStruct(q.shape, jnp.bfloat16),
        in_specs=[far_spec] * 4,
        out_specs=pl.BlockSpec(memory_space=pl.ANY),
        scratch_shapes=[
            pltpu.SMEM(lengths.shape, jnp.int32),
            pltpu.VMEM((SIDE, ROWS, WIDE), jnp.bfloat16),
            pltpu.VMEM(((REACH + 1) * SIDE, 2, ROWS, HEAD), jnp.bfloat16),
            pltpu.VMEM((SIDE, ROWS, LANES), jnp.int32),
            pltpu.VMEM((SIDE, WIDE, LANES), jnp.float32),
            pltpu.VMEM((SIDE, WIDE, LANES), jnp.float32),
            pltpu.VMEM((SIDE, WIDE, HEAD), jnp.float32),
            pltpu.VMEM((SIDE, ROWS, WIDE), jnp.bfloat16),
            dma((4,)), dma((9,)), dma((9,)), dma((REACH, SIDE)), dma((REACH, SIDE)), dma((3, SIDE)), dma((3, SIDE)),
        ],
        compiler_params=pltpu.CompilerParams(
            collective_id=0, has_side_effects=True, vmem_limit_bytes=32 * 1024 * 1024
        ),
        name="attention",
    )(lengths, q, k, v)


def solution(mesh):
    in_specs = (P(("dp", "ctx"), None), P(("dp", "ctx"), None), P(("dp", "ctx"), None), P("dp"))
    out_specs = P(("dp", "ctx"), None)
    return jax.shard_map(body, mesh=mesh, in_specs=in_specs, out_specs=out_specs, check_vma=False)
```

time: 49 us -> 33.5 us (0.68)
  the two profiles are of different devices: /device:TPU:56 before, /device:TPU:376 now
where the time goes in v2:
time: 33.5 us; the launch traced here: 33.4 us
  Pallas kernels  32.6 us (97%)
  local copies, waits for them, and re-layouts  0.8 us (2%)
    pallas_call x1, Pallas kernels, body(): pl.pallas_call(kernel, out_shape=jax.ShapeDtypeStruct(q.shape, jnp.bfloat...  32.6 us
    unnamed x1, local copies, waits for them, and re-layouts  0.8 us

profile of v2, /device:TPU:376, one launch (start us, length us, event | category | flops | bytes accessed | tf_op | source)
XLA Modules:
  0.0 33.4 jit_solution(7348286127341803060)
XLA Ops:
  0.0 32.6 %attention.1 = bf16[128,2048]{1,0:T(8,128)(2,1)S(1)} custom-call(s32[16]{0:T(128)} %lengths_hbm.1, bf16[128,2048]{1,0:T(8,128)(2,1)} %q_hbm.1, bf16[128,512]{1,0:T(8,128)(2,1)} %k_hbm.1, bf16[128,512]{1,0:T(8,128)(2,1)} %v_hbm.1), custom_call_target="tpu_custom_call" | custom-call | tf_op jit(solution)/shard_map/attention/pallas_call | solution.py:276
  32.6 0.8 %copy.6 = bf16[128,2048]{1,0:T(8,128)(2,1)} copy(bf16[128,2048]{1,0:T(8,128)(2,1)S(1)} %attention.1) | data formatting | bytes 1048576

commit v3 on v2

--- a/solution.py
+++ b/solution.py
@@ -44,8 +44,6 @@
         pltpu.make_async_copy(lengths_hbm, lengths, loc_sem.at[2]),
         pltpu.make_async_copy(cols(q_hbm, x, WIDE), q_buf.at[x], loc_sem.at[3]),
     ]
-    for copy in local:
-        copy.start()
 
     barrier = pltpu.get_barrier_semaphore()
 
@@ -57,6 +55,8 @@
     pl.when(z > 0)(lambda: greet(below))
     pl.when(z < depth - 1)(lambda: greet(above))
 
+    for copy in local:
+        copy.start()
     pl.semaphore_wait(barrier, 3 + jnp.where(z > 0, 1, 0) + jnp.where(z < depth - 1, 1, 0))
 
     def remote(src, dst, send, recv, to):
@@ -144,11 +144,11 @@
     for copy in kv_out["left"]:
         copy.wait_recv()
     hops[0][2].start()
-    for copy in q_out.values():
-        copy.start()
     for copy in kv_out["far"]:
         copy.wait_recv()
     hops[0][3].start()
+    for copy in q_out.values():
+        copy.start()
     for slot in (0, 1):
         hops[0][slot].wait_recv()
         hops[1][slot].start()

time: 33.5 us -> 33.1 us (0.988)
  the two profiles are of different devices: /device:TPU:376 before, /device:TPU:352 now
where the time goes in v3:
time: 33.1 us; the launch traced here: 33 us
  Pallas kernels  32.2 us (97%)
  local copies, waits for them, and re-layouts  0.8 us (2%)
    pallas_call x1, Pallas kernels, body(): pl.pallas_call(kernel, out_shape=jax.ShapeDtypeStruct(q.shape, jnp.bfloat...  32.2 us
    unnamed x1, local copies, waits for them, and re-layouts  0.8 us

profile of v3, /device:TPU:352, one launch (start us, length us, event | category | flops | bytes accessed | tf_op | source)
XLA Modules:
  0.0 33.0 jit_solution(15996956141932530251)
XLA Ops:
  0.0 32.2 %attention.1 = bf16[128,2048]{1,0:T(8,128)(2,1)S(1)} custom-call(s32[16]{0:T(128)} %lengths_hbm.1, bf16[128,2048]{1,0:T(8,128)(2,1)} %q_hbm.1, bf16[128,512]{1,0:T(8,128)(2,1)} %k_hbm.1, bf16[128,512]{1,0:T(8,128)(2,1)} %v_hbm.1), custom_call_target="tpu_custom_call" | custom-call | tf_op jit(solution)/shard_map/attention/pallas_call | solution.py:276
  32.2 0.8 %copy.6 = bf16[128,2048]{1,0:T(8,128)(2,1)} copy(bf16[128,2048]{1,0:T(8,128)(2,1)S(1)} %attention.1) | data formatting | bytes 1048576

commit v4 on v3

--- a/solution.py
+++ b/solution.py
@@ -57,6 +57,19 @@
 
     for copy in local:
         copy.start()
+    def clear(b, carry):
+        top[b] = jnp.full((WIDE, LANES), LOWEST, jnp.float32)
+        total[b] = jnp.zeros((WIDE, LANES), jnp.float32)
+        acc[b] = jnp.zeros((WIDE, HEAD), jnp.float32)
+        return carry
+
+    lax.fori_loop(0, SIDE, clear, 0)
+
+    def blank(i, carry):
+        kv[i] = jnp.zeros((2, ROWS, HEAD), jnp.bfloat16)
+        return carry
+
+    lax.fori_loop(0, SIDE * jnp.maximum(REACH - z, 0), blank, 0)
     pl.semaphore_wait(barrier, 3 + jnp.where(z > 0, 1, 0) + jnp.where(z < depth - 1, 1, 0))
 
     def remote(src, dst, send, recv, to):
@@ -112,19 +125,6 @@
     local[0].wait()
     local[1].wait()
     hops[0][0].start()
-    def clear(b, carry):
-        top[b] = jnp.full((WIDE, LANES), LOWEST, jnp.float32)
-        total[b] = jnp.zeros((WIDE, LANES), jnp.float32)
-        acc[b] = jnp.zeros((WIDE, HEAD), jnp.float32)
-        return carry
-
-    lax.fori_loop(0, SIDE, clear, 0)
-
-    def blank(i, carry):
-        kv[i] = jnp.zeros((2, ROWS, HEAD), jnp.bfloat16)
-        return carry
-
-    lax.fori_loop(0, SIDE * jnp.maximum(REACH - z, 0), blank, 0)
     local[2].wait()
 
     def starts(b, carry):

time: 33.1 us -> 33.1 us (level)
  the two profiles are of different devices: /device:TPU:352 before, /device:TPU:376 now
where the time goes in v4:
time: 33.1 us; the launch traced here: 33 us
  Pallas kernels  32.2 us (97%)
  local copies, waits for them, and re-layouts  0.8 us (2%)
    pallas_call x1, Pallas kernels, body(): pl.pallas_call(kernel, out_shape=jax.ShapeDtypeStruct(q.shape, jnp.bfloat...  32.2 us
    unnamed x1, local copies, waits for them, and re-layouts  0.8 us

profile of v4, /device:TPU:376, one launch (start us, length us, event | category | flops | bytes accessed | tf_op | source)
XLA Modules:
  0.0 33.0 jit_solution(6522327480820429967)
XLA Ops:
  0.0 32.2 %attention.1 = bf16[128,2048]{1,0:T(8,128)(2,1)S(1)} custom-call(s32[16]{0:T(128)} %lengths_hbm.1, bf16[128,2048]{1,0:T(8,128)(2,1)} %q_hbm.1, bf16[128,512]{1,0:T(8,128)(2,1)} %k_hbm.1, bf16[128,512]{1,0:T(8,128)(2,1)} %v_hbm.1), custom_call_target="tpu_custom_call" | custom-call | tf_op jit(solution)/shard_map/attention/pallas_call | solution.py:276
  32.2 0.8 %copy.6 = bf16[128,2048]{1,0:T(8,128)(2,1)} copy(bf16[128,2048]{1,0:T(8,128)(2,1)S(1)} %attention.1) | data formatting | bytes 1048576

commit v5 on v4

--- a/solution.py
+++ b/solution.py
@@ -166,7 +166,9 @@
         key_pos = start + lax.broadcasted_iota(jnp.int32, (ROWS, n), 1)
         allowed = key_pos >= jnp.concatenate([lo_ref[b]] * pieces, axis=1)
         if causal:
-            allowed = allowed & (key_pos <= (base + b) * ROWS + lax.broadcasted_iota(jnp.int32, (ROWS, n), 0))
+            early = n - SIDE * ROWS
+            q_pos = (base + b) * ROWS + lax.broadcasted_iota(jnp.int32, (ROWS, SIDE * ROWS), 0)
+            allowed = jnp.concatenate([allowed[:, :early], allowed[:, early:] & (key_pos[:, early:] <= q_pos)], axis=1)
         olds = [(top[b, at], total[b, at], acc[b, at]) for at in heads]
         news = []
         for h, (old_top, old_total, old_acc) in enumerate(olds):

time: 33.1 us -> 33.1 us (level)
  no operation moved by 1% of the time
where the time goes in v5:
time: 33.1 us; the launch traced here: 33 us
  Pallas kernels  32.2 us (97%)
  local copies, waits for them, and re-layouts  0.8 us (2%)
    pallas_call x1, Pallas kernels, body(): pl.pallas_call(kernel, out_shape=jax.ShapeDtypeStruct(q.shape, jnp.bfloat...  32.2 us
    unnamed x1, local copies, waits for them, and re-layouts  0.8 us

profile of v5, /device:TPU:376, one launch (start us, length us, event | category | flops | bytes accessed | tf_op | source)
XLA Modules:
  0.0 33.0 jit_solution(16018197512196148314)
XLA Ops:
  0.0 32.2 %attention.1 = bf16[128,2048]{1,0:T(8,128)(2,1)S(1)} custom-call(s32[16]{0:T(128)} %lengths_hbm.1, bf16[128,2048]{1,0:T(8,128)(2,1)} %q_hbm.1, bf16[128,512]{1,0:T(8,128)(2,1)} %k_hbm.1, bf16[128,512]{1,0:T(8,128)(2,1)} %v_hbm.1), custom_call_target="tpu_custom_call" | custom-call | tf_op jit(solution)/shard_map/attention/pallas_call | solution.py:278
  32.2 0.8 %copy.6 = bf16[128,2048]{1,0:T(8,128)(2,1)} copy(bf16[128,2048]{1,0:T(8,128)(2,1)S(1)} %attention.1) | data formatting | bytes 1048576
